TPU v7x, 32 devices: a whole 2x2x4 slice. The times are simulated.
32 devices in a mesh: wide: 4 (over y, core), narrow: 8 (over z, x).
Axes of the slice: x: 2, y: 2, z: 4, core: 2. Of those that a mesh axis runs over, the one named last changes fastest.
Arguments:
- leaf_rhs: bfloat16 [64, 1024, 256], P('wide', 'narrow'), may hold values from -6 to 6
- leaf_inv: bfloat16 [64, 256, 256], P('wide', 'narrow'), may hold values from -0.375 to 0.375
- leaf_upd: bfloat16 [64, 5, 256, 256], P('wide', None, 'narrow'), may hold values from -0.0390625 to 0.0390625
- leaf_targets: int32 [64, 5], P('wide'), may hold values from 0 to 2
- sep_rhs: bfloat16 [3, 1024, 256], P(None, 'narrow'), may hold values from -6 to 6
- sep_inv: bfloat16 [3, 256, 256], replicated, may hold values from -0.375 to 0.375
- sep_low: bfloat16 [3, 256, 256], replicated, may hold values from -0.21875 to 0.21875
Outputs:
- leaf_sol: bfloat16 [64, 1024, 256], P('wide', 'narrow')
- sep_sol: bfloat16 [3, 1024, 256], P(None, 'narrow')
All inputs are finite; a program needn't handle non-finite values.
Results may differ from a plain program's by a relative error of at most 0.012.
Values may be sent and summed in bfloat16 or wider, within the bound.
A program may use at most 64 MiB of HBM per device.

v0:
```python
import jax
import jax.numpy as jnp
from jax import lax
from jax.sharding import PartitionSpec as P


def separator_solve(gathered, sep_rhs, sep_inv, sep_low):
    nsep = sep_inv.shape[0]
    solved_list = []
    for row in range(nsep):
        reduced = sep_rhs[row].astype(jnp.float32) - gathered[row]
        for col in range(row):
            reduced = reduced - jnp.dot(
                solved_list[col],
                sep_low[row * (row - 1) // 2 + col],
                preferred_element_type=jnp.float32,
            )
        reduced = reduced.astype(jnp.bfloat16)
        solved_list.append(
            jnp.dot(reduced, sep_inv[row], preferred_element_type=jnp.float32).astype(jnp.bfloat16)
        )
    return jnp.stack(solved_list)


def body(leaf_rhs, leaf_inv, leaf_upd, leaf_targets, sep_rhs, sep_inv, sep_low):
    nsep = sep_inv.shape[0]
    nupd = leaf_upd.shape[1]
    leaves, scenarios, width = leaf_rhs.shape
    onehot = (leaf_targets[:, :, None] == jnp.arange(nsep, dtype=jnp.int32)[None, None, :]).astype(
        jnp.float32
    )
    columns = leaf_rhs
    leaf_sol = jnp.einsum(
        "lcj,lji->lci",
        columns,
        lax.all_gather(leaf_inv, "narrow", axis=1, tiled=True),
        preferred_element_type=jnp.float32,
    ).astype(jnp.bfloat16)
    start_sum = jnp.zeros((nsep, scenarios, width), jnp.float32)
    total = start_sum
    piece = lax.all_gather(leaf_upd, "narrow", axis=2, tiled=True)
    columns = leaf_sol
    for block in range(nupd):
        contrib = jnp.einsum(
            "lcj,lji->lci", columns, piece[:, block], preferred_element_type=jnp.float32
        )
        total = total + jnp.einsum("lci,ls->sci", contrib, onehot[:, block])
    gathered = total
    total = lax.psum(gathered, "wide")
    sep_sol = separator_solve(total, sep_rhs, sep_inv, sep_low)
    return (leaf_sol, sep_sol)


def solution(mesh):
    in_specs = (
        P("wide", "narrow", None),
        P("wide", "narrow", None),
        P("wide", None, "narrow", None),
        P("wide", None),
        P(None, "narrow", None),
        P(),
        P(),
    )
    out_specs = (P("wide", "narrow", None), P(None, "narrow", None))
    return jax.shard_map(body, mesh=mesh, in_specs=in_specs, out_specs=out_specs, check_vma=False)
```

profile of v0, /device:TPU:0, one launch (start us, length us, event | category | flops | bytes accessed | tf_op | source)
XLA Modules:
  0.0 266.1 jit_solution(2337355595048886722)
XLA Ops:
  7.2 0.0 copy-start
  7.2 0.0 all-gather.3.cloned.1.call-start
  7.2 0.7 all-gather.3.cloned.1.call-update
  7.9 0.0 all-gather.5.cloned.1.call-start
  8.0 0.7 all-gather.5.cloned.1.call-update
  8.7 0.0 all-reduce.2.cloned.1.call-start
  8.7 0.7 iota_compare_fusion
  9.4 52.8 %all-gather.3.cloned.1.call-done = bf16[16,256,256]{2,1,0:T(8,128)(2,1)} async-done(((bf16[16,32,256]{2,1,0:T(8,128)(2,1)}), bf16[16,256,256]{2,1,0:T(8,128)(2,1)}) %all-gather.3.cloned.1.call-update) | async-done | bytes 2097168 | tf_op jit(solution)/shard_map/all_gather | solution.py:36
  62.2 0.0 copy-done
  62.2 2.0 convolution_convert_fusion
  64.2 0.0 copy-start.1
  64.3 149.5 %all-gather.5.cloned.1.call-done = bf16[16,5,256,256]{3,2,1,0:T(8,128)(2,1)} async-done(((bf16[16,5,32,256]{3,2,1,0:T(8,128)(2,1)}), bf16[16,5,256,256]{3,2,1,0:T(8,128)(2,1)}) %all-gather.5.cloned.1.call-update) | async-done | bytes 10485776 | tf_op jit(solution)/shard_map/all_gather | solution.py:41
  213.8 0.0 copy-start.2
  213.8 2.2 fusion.3
  216.0 0.7 fusion.11
  216.6 2.7 %fusion.1 = bf16[16,128,256]{2,1,0:T(8,128)(2,1)S(1)} fusion(bf16[16,128,256]{2,1,0:T(8,128)(2,1)S(1)} %convolution_convert_fusion, bf16[16,5,256,256]{3,2,1,0:T(8,128)(2,1)} %all-gather.5.cloned.1.call-done), kind=kOutput, calls=%fused_computation.3 | convolution fusion | flops 268435456 | bytes 4194304 | tf_op jit(solution)/shard_map/lcj,lji->lci/dot_general | solution.py:44
  219.4 0.7 fusion.7
  220.1 0.0 copy-done.2
  220.1 0.5 fusion.2
  220.5 0.7 fusion.9
  221.2 0.5 fusion.4
  221.7 0.8 fusion.21
  222.4 0.0 copy-done.1
  222.4 0.5 fusion
  222.9 0.0 copy-start.5
  222.9 0.0 copy-start.4
  222.9 0.0 copy-start.3
  222.9 1.5 fusion.24
  224.4 0.0 all-reduce.2.cloned.1.call-update
  224.4 0.0 copy-done.5
  224.5 31.5 %all-reduce.2.cloned.1.call-done = f32[3,128,256]{2,0,1:T(4,128)} async-done(((f32[3,128,256]{2,0,1:T(4,128)}), f32[3,128,256]{2,0,1:T(4,128)}) %all-reduce.2.cloned.1.call-update) | async-done | bytes 393232 | tf_op jit(solution)/shard_map/psum | solution.py:49
  256.0 1.9 slice_subtract_fusion.1
  257.9 0.0 copy-done.4
  257.9 0.2 convolution_convert_fusion.3
  258.1 0.0 copy-done.3
  258.1 0.3 convolution_convert_fusion.2
  258.4 0.2 convolution_subtract_fusion.1
  258.6 0.3 fusion.29
  258.9 0.7 pad_maximum_fusion
  (1 shorter events, 0.0 us)
Async XLA Ops:
  7.2 55.0 %copy-start = (bf16[16,128,256]{2,1,0:T(8,128)(2,1)S(1)}, bf16[16,128,256]{2,1,0:T(8,128)(2,1)}, u32[]{:S(2)}) copy-start(bf16[16,128,256]{2,1,0:T(8,128)(2,1)} %param.7) | copy-start | bytes 3145732
  7.2 55.0 %all-gather.3.cloned.1.call-start = ((), (), s32[]{:S(2)}) async-start(), calls=%async_computation | async-start | bytes 2359296 | tf_op jit(solution)/shard_map/all_gather | solution.py:36
  7.9 205.8 %all-gather.5.cloned.1.call-start = ((), (), s32[]{:S(2)}) async-start(), calls=%async_computation.1 | async-start | bytes 11796480 | tf_op jit(solution)/shard_map/all_gather | solution.py:41
  8.7 247.4 %all-reduce.2.cloned.1.call-start = ((), (), s32[]{:S(2)}) async-start(), calls=%async_computation.2 | async-start | bytes 1048576 | tf_op jit(solution)/shard_map/psum | solution.py:49
  64.2 158.2 %copy-start.1 = (bf16[16,128,256]{2,1,0:T(8,128)(2,1)}, bf16[16,128,256]{2,1,0:T(8,128)(2,1)S(1)}, u32[]{:S(2)}) copy-start(bf16[16,128,256]{2,1,0:T(8,128)(2,1)S(1)} %convolution_convert_fusion) | copy-start | bytes 3145732
  213.8 6.3 %copy-start.2 = (bf16[16,5,256,256]{3,2,1,0:T(8,128)(2,1)S(1)}, bf16[16,5,256,256]{3,2,1,0:T(8,128)(2,1)}, u32[]{:S(2)}) copy-start(bf16[16,5,256,256]{3,2,1,0:T(8,128)(2,1)} %all-gather.5.cloned.1.call-done) | copy-start | bytes 31457284
  222.9 1.6 copy-start.5
  222.9 35.0 %copy-start.4 = (bf16[3,256,256]{2,1,0:T(8,128)(2,1)S(1)}, bf16[3,256,256]{2,1,0:T(8,128)(2,1)}, u32[]{:S(2)}) copy-start(bf16[3,256,256]{2,1,0:T(8,128)(2,1)} %param.12) | copy-start | bytes 1179652
  222.9 35.2 %copy-start.3 = (bf16[3,256,256]{2,1,0:T(8,128)(2,1)S(1)}, bf16[3,256,256]{2,1,0:T(8,128)(2,1)}, u32[]{:S(2)}) copy-start(bf16[3,256,256]{2,1,0:T(8,128)(2,1)} %param.13) | copy-start | bytes 1179652
Sparse Core Ops, SparseCore 0:
  10.2 51.9 all-gather.2
  64.4 149.3 all-gather.4
  224.6 31.4 all-reduce.1
where the time goes:
time: 266 us
  waiting for transfers between devices  235 us (88%)
  between operations  13.9 us (5%)
  matrix products  13.5 us (5%)
  other arithmetic  3.29 us (1%)
    all_gather x1, waiting for transfers between devices, body(): piece = lax.all_gather(leaf_upd, 'narrow', axis=2, tiled=True)  150 us
    all_gather x1, waiting for transfers between devices, body(): lax.all_gather(leaf_inv, 'narrow', axis=1, tiled=True)  52.8 us
    psum x1, waiting for transfers between devices, body(): total = lax.psum(gathered, 'wide')  31.5 us
    dot_general x5, matrix products, body(): jnp.einsum('lcj,lji->lci', columns, piece[:, block], preferred_element_ty...  6.28 us
  transfers between devices with their start and end apart: 3, of which 3 were waited for; matrix products, arithmetic and copies ran while one was open for 1% of the time, Pallas kernels for 0%

commit v1 on v0

--- a/solution.py
+++ b/solution.py
@@ -46,7 +46,7 @@
         )
         total = total + jnp.einsum("lci,ls->sci", contrib, onehot[:, block])
     gathered = total
-    total = lax.psum(gathered, "wide")
+    total = jnp.sum(lax.all_gather(gathered, "wide"), axis=0)
     sep_sol = separator_solve(total, sep_rhs, sep_inv, sep_low)
     return (leaf_sol, sep_sol)
 

time: 266 us -> 252 us (0.947)
  waiting for transfers between devices: 235 us -> 220 us
  local copies, waits for them, and re-layouts: 0.05 us -> 3.4 us
    psum x1 -> x0, waiting for transfers between devices: 31.5 us -> none  [body(): total = lax.psum(gathered, 'wide')]
    all_gather x0 -> x1, waiting for transfers between devices: none -> 18 us  [body(): total = jnp.sum(lax.all_gather(gathered, 'wide'), axis=0)]
  transfers between devices with their start and end apart: 3 -> 3, of which waited for: 3 -> 3; matrix products, arithmetic and copies ran while one was open for 1% -> 2% of each run, Pallas kernels for 0% -> 0%
where the time goes in v1:
time: 252 us
  waiting for transfers between devices  220 us (87%)
  between operations  13.9 us (6%)
  matrix products  12.7 us (5%)
  local copies, waits for them, and re-layouts  3.4 us (1%)
    all_gather x1, waiting for transfers between devices, body(): piece = lax.all_gather(leaf_upd, 'narrow', axis=2, tiled=True)  150 us
    all_gather x1, waiting for transfers between devices, body(): lax.all_gather(leaf_inv, 'narrow', axis=1, tiled=True)  51.6 us
    all_gather x1, waiting for transfers between devices, body(): total = jnp.sum(lax.all_gather(gathered, 'wide'), axis=0)  18 us
    dot_general x5, matrix products, body(): jnp.einsum('lcj,lji->lci', columns, piece[:, block], preferred_element_ty...  6.28 us
  transfers between devices with their start and end apart: 3, of which 3 were waited for; matrix products, arithmetic and copies ran while one was open for 2% of the time, Pallas kernels for 0%

profile of v1, /device:TPU:0, one launch (start us, length us, event | category | flops | bytes accessed | tf_op | source)
XLA Modules:
  0.0 252.2 jit_solution(10051852700081317178)
XLA Ops:
  7.2 0.0 copy-start
  7.2 0.0 copy-start.6
  7.2 0.0 all-gather.5.cloned.1.call-start
  7.2 0.7 all-gather.5.cloned.1.call-update
  7.9 0.0 all-gather.7.cloned.1.call-start
  8.0 2.6 %copy.10 = bf16[16,5,32,256]{3,2,0,1:T(8,128)(2,1)} copy(bf16[16,5,32,256]{3,2,1,0:T(8,128)(2,1)} %param.9) | data formatting | bytes 2621440 | tf_op args[2]
  10.5 0.0 all-gather.7.cloned.1.call-update
  10.5 0.0 all-gather.9.cloned.1.call-start
  10.6 0.0 copy-done.6
  10.6 51.6 %all-gather.5.cloned.1.call-done = bf16[16,256,256]{2,1,0:T(8,128)(2,1)} async-done(((bf16[16,32,256]{2,1,0:T(8,128)(2,1)}), bf16[16,256,256]{2,1,0:T(8,128)(2,1)}) %all-gather.5.cloned.1.call-update) | async-done | bytes 2097168 | tf_op jit(solution)/shard_map/all_gather | solution.py:36
  62.2 0.0 copy-done
  62.2 2.0 convolution_convert_fusion
  64.3 0.0 copy-start.1
  64.3 149.5 %all-gather.7.cloned.1.call-done = bf16[16,5,256,256]{3,2,0,1:T(8,128)(2,1)} async-done(((bf16[16,5,32,256]{3,2,0,1:T(8,128)(2,1)}), bf16[16,5,256,256]{3,2,0,1:T(8,128)(2,1)}) %all-gather.7.cloned.1.call-update) | async-done | bytes 10485776 | tf_op jit(solution)/shard_map/all_gather | solution.py:41
  213.8 0.0 copy-start.2
  213.8 2.2 fusion.3
  216.0 0.7 fusion.11
  216.6 2.7 %fusion.1 = bf16[16,128,256]{2,1,0:T(8,128)(2,1)S(1)} fusion(bf16[16,128,256]{2,1,0:T(8,128)(2,1)S(1)} %convolution_convert_fusion, bf16[16,5,256,256]{3,2,0,1:T(8,128)(2,1)} %all-gather.7.cloned.1.call-done), kind=kOutput, calls=%fused_computation.3 | convolution fusion | flops 268435456 | bytes 4194304 | tf_op jit(solution)/shard_map/lcj,lji->lci/dot_general | solution.py:44
  219.4 0.7 fusion.7
  220.1 0.0 copy-done.2
  220.1 0.5 fusion.2
  220.5 0.7 fusion.9
  221.2 0.5 fusion.4
  221.7 0.8 fusion.21
  222.4 0.0 copy-done.1
  222.4 0.5 fusion
  222.9 0.7 fusion.24
  223.6 0.0 copy-start.3
  223.6 0.0 copy-start.5
  223.6 0.0 copy-start.4
  223.6 0.8 copy.16
  224.4 0.0 all-gather.9.cloned.1.call-update
  224.4 18.0 %all-gather.9.cloned.1.call-done = f32[12,128,256]{2,1,0:T(8,128)} async-done(((f32[3,128,256]{2,1,0:T(8,128)}), f32[12,128,256]{2,1,0:T(8,128)}) %all-gather.9.cloned.1.call-update) | async-done | bytes 1572880 | tf_op jit(solution)/shard_map/all_gather | solution.py:49
  242.4 1.6 reduce_sum.9
  244.0 0.0 copy-done.3
  244.0 0.0 copy-done.5
  244.0 0.2 convolution_convert_fusion.3
  244.2 0.0 copy-done.4
  244.2 0.3 convolution_convert_fusion.2
  244.5 0.2 convolution_subtract_fusion.1
  244.7 0.3 fusion.29
  245.0 0.7 pad_maximum_fusion
  (1 shorter events, 0.0 us)
Async XLA Ops:
  7.2 55.0 %copy-start = (bf16[16,128,256]{2,1,0:T(8,128)(2,1)S(1)}, bf16[16,128,256]{2,1,0:T(8,128)(2,1)}, u32[]{:S(2)}) copy-start(bf16[16,128,256]{2,1,0:T(8,128)(2,1)} %param.7) | copy-start | bytes 3145732
  7.2 3.4 %copy-start.6 = (s32[16,5]{0,1:T(8,128)S(1)}, s32[16,5]{0,1:T(8,128)}, u32[]{:S(2)}) copy-start(s32[16,5]{0,1:T(8,128)} %param.10) | copy-start | bytes 964
  7.2 55.0 %all-gather.5.cloned.1.call-start = ((), (), s32[]{:S(2)}) async-start(), calls=%async_computation | async-start | bytes 2359296 | tf_op jit(solution)/shard_map/all_gather | solution.py:36
  7.9 205.8 %all-gather.7.cloned.1.call-start = ((), (), s32[]{:S(2)}) async-start(), calls=%async_computation.1 | async-start | bytes 11796480 | tf_op jit(solution)/shard_map/all_gather | solution.py:41
  10.5 231.9 %all-gather.9.cloned.1.call-start = ((), (), s32[]{:S(2)}) async-start(), calls=%async_computation.2 | async-start | bytes 1966080 | tf_op jit(solution)/shard_map/all_gather | solution.py:49
  64.3 158.2 %copy-start.1 = (bf16[16,128,256]{2,1,0:T(8,128)(2,1)}, bf16[16,128,256]{2,1,0:T(8,128)(2,1)S(1)}, u32[]{:S(2)}) copy-start(bf16[16,128,256]{2,1,0:T(8,128)(2,1)S(1)} %convolution_convert_fusion) | copy-start | bytes 3145732
  213.8 6.3 %copy-start.2 = (bf16[16,5,256,256]{3,2,0,1:T(8,128)(2,1)S(1)}, bf16[16,5,256,256]{3,2,0,1:T(8,128)(2,1)}, u32[]{:S(2)}) copy-start(bf16[16,5,256,256]{3,2,0,1:T(8,128)(2,1)} %all-gather.7.cloned.1.call-done) | copy-start | bytes 31457284
  223.6 20.4 %copy-start.3 = (bf16[3,256,256]{2,1,0:T(8,128)(2,1)S(1)}, bf16[3,256,256]{2,1,0:T(8,128)(2,1)}, u32[]{:S(2)}) copy-start(bf16[3,256,256]{2,1,0:T(8,128)(2,1)} %param.12) | copy-start | bytes 1179652
  223.6 20.4 %copy-start.5 = (bf16[3,128,256]{2,1,0:T(8,128)(2,1)S(1)}, bf16[3,128,256]{2,1,0:T(8,128)(2,1)}, u32[]{:S(2)}) copy-start(bf16[3,128,256]{2,1,0:T(8,128)(2,1)} %param.11) | copy-start | bytes 589828
  223.6 20.6 %copy-start.4 = (bf16[3,256,256]{2,1,0:T(8,128)(2,1)S(1)}, bf16[3,256,256]{2,1,0:T(8,128)(2,1)}, u32[]{:S(2)}) copy-start(bf16[3,256,256]{2,1,0:T(8,128)(2,1)} %param.13) | copy-start | bytes 1179652
Sparse Core Ops, SparseCore 0:
  10.2 51.9 all-gather.4
  64.4 149.3 all-gather.6
  224.6 17.8 all-gather.8
